TPU v7x, 32 devices: a whole 2x2x4 slice. The times are simulated.
32 devices in a mesh: variant: 4 (over y, x), vocab: 8 (over z, core).
Axes of the slice: x: 2, y: 2, z: 4, core: 2. Of those that a mesh axis runs over, the one named last changes fastest.
Arguments:
- teacher_hidden: bfloat16 [4, 256, 4096], P(None, None, ('variant', 'vocab')), may hold values from -24 to 24
- teacher_weight: bfloat16 [4096, 64128], P(None, ('vocab', 'variant')), may hold values from -1 to 1
- variant_ids: int32 [4], replicated, may hold values from 0 to 13
- temps: float32 [14], replicated, may hold values from 0.7 to 1.5
- student_hidden: bfloat16 [256, 2048], P(None, 'variant'), may hold values from -24 to 24
- student_weight: bfloat16 [2048, 64128], P('variant', 'vocab'), may hold values from -1 to 1
- token_ids: int32 [256], P('variant'), may hold values from 0 to 64127
- loss_mask: int32 [256], P('variant'), may hold values 0 or 1
Outputs:
- token_loss: float32 [256], P('variant')
- student_grad: float32 [2048, 64128], P('variant', 'vocab')
All inputs are finite; a program needn't handle non-finite values. No bound on the sum of `loss_mask` on one device may be relied on, other than what follows from the above.
Results may differ from a plain program's by a relative error of at most 0.0025.
Values may be sent and summed in bfloat16 or wider, within the bound.
A program may use at most 192 MiB of HBM per device.

v0:
```python
import jax
import jax.numpy as jnp
from jax import lax
from jax.sharding import PartitionSpec as P

mix_weight = 0.5
loss_scale = 4096.0


def on_device(
    teacher_hidden,
    teacher_weight,
    variant_ids,
    temps,
    student_hidden,
    student_weight,
    token_ids,
    loss_mask,
):
    n_variant = lax.axis_size("variant")
    categories = jnp.arange(temps.shape[0], dtype=jnp.int32)
    taus = jnp.sum(
        jnp.where(variant_ids[:, None] == categories[None, :], temps[None, :], 0.0), axis=1
    )
    hidden_all = lax.all_gather(teacher_hidden, ("variant", "vocab"), axis=2, tiled=True)
    scaled = (
        jnp.einsum("vtd,dc->vtc", hidden_all, teacher_weight, preferred_element_type=jnp.float32)
        / taus[:, None, None]
    )
    local_max = jnp.max(scaled, axis=2)
    top = lax.pmax(local_max, ("variant", "vocab"))
    total = lax.psum(jnp.sum(jnp.exp(scaled - top[:, :, None]), axis=2), ("variant", "vocab"))
    probs = jnp.exp(scaled - top[:, :, None]) / total[:, :, None]
    averaged_cols = jnp.sum(probs, axis=0) / n_variant
    averaged = lax.all_to_all(
        averaged_cols.astype(jnp.bfloat16), "variant", split_axis=0, concat_axis=1, tiled=True
    ).astype(averaged_cols.dtype)
    block = student_hidden
    logits = lax.psum_scatter(
        jnp.dot(block, student_weight, preferred_element_type=jnp.float32),
        "variant",
        scatter_dimension=0,
        tiled=True,
    )
    local_max = jnp.max(logits, axis=1)
    top = lax.pmax(local_max, "vocab")
    total = lax.psum(jnp.sum(jnp.exp(logits - top[:, None]), axis=1), "vocab")
    log_probs = logits - (top + jnp.log(total))[:, None]
    probs_student = jnp.exp(log_probs)
    columns = lax.axis_index("vocab") * logits.shape[1] + jnp.arange(
        logits.shape[1], dtype=jnp.int32
    )
    onehot = token_ids[:, None] == columns[None, :]
    soft, hard = lax.psum(
        (jnp.sum(averaged * log_probs, axis=1), jnp.sum(jnp.where(onehot, log_probs, 0.0), axis=1)),
        "vocab",
    )
    maskf = loss_mask.astype(jnp.float32)
    token_loss = maskf * (-mix_weight * soft - (1.0 - mix_weight) * hard)
    error = (
        loss_scale
        * maskf[:, None]
        * (probs_student - mix_weight * averaged - (1.0 - mix_weight) * onehot.astype(jnp.float32))
    ).astype(jnp.bfloat16)
    block = student_hidden
    student_grad = lax.dot_general(
        block,
        lax.all_gather(error, "variant", axis=0, tiled=True),
        (((0,), (0,)), ((), ())),
        preferred_element_type=jnp.float32,
    )
    return (token_loss, student_grad)


def solution(mesh):
    in_specs = (
        P(None, None, ("variant", "vocab")),
        P(None, ("vocab", "variant")),
        P(),
        P(),
        P(None, "variant"),
        P("variant", "vocab"),
        P("variant"),
        P("variant"),
    )
    out_specs = (P("variant"), P("variant", "vocab"))
    return jax.shard_map(
        on_device, mesh=mesh, in_specs=in_specs, out_specs=out_specs, check_vma=False
    )
```

profile of v0, /device:TPU:0, one launch (start us, length us, event | category | flops | bytes accessed | tf_op | source)
XLA Modules:
  0.0 342.5 jit_solution(14589782983630050542)
XLA Ops:
  8.0 0.0 copy-start
  8.0 0.0 all-gather.3.cloned.1.call-start
  8.1 0.7 all-gather.3.cloned.1.call-update
  8.7 0.0 reduce-scatter.2.cloned.1.call-start
  8.8 0.2 copy-done
  9.0 9.1 %fusion.10 = f32[256,8016]{1,0:T(8,128)} fusion(bf16[256,512]{1,0:T(8,128)(2,1)S(1)} %copy-done, bf16[512,8016]{0,1:T(8,128)(2,1)} %param.13), kind=kOutput, calls=%fused_computation.24 | convolution fusion | flops 2101346304 | bytes 16678912 | tf_op jit(solution)/shard_map/dot_general | solution.py:40
  18.0 0.0 copy-start.4
  18.0 0.0 copy-start.5
  18.0 0.0 reduce-scatter.2.cloned.1.call-update
  18.0 0.6 copy-done.4
  18.7 0.0 copy-done.5
  18.7 0.2 select_reduce_fusion
  18.9 94.8 %all-gather.3.cloned.1.call-done = bf16[4,256,4096]{2,1,0:T(8,128)(2,1)} async-done(((bf16[4,256,128]{2,1,0:T(8,128)(2,1)}), bf16[4,256,4096]{2,1,0:T(8,128)(2,1)}) %all-gather.3.cloned.1.call-update) | async-done | bytes 8388624 | tf_op jit(solution)/shard_map/all_gather | solution.py:25
  113.6 24.0 %fusion.9 = (f32[4,256]{1,0:T(4,128)S(1)}, f32[4,256,2004]{1,2,0:T(8,128)}) fusion(f32[4]{0:T(128)S(1)} %select_reduce_fusion, bf16[4,256,4096]{2,1,0:T(8,128)(2,1)} %all-gather.3.cloned.1.call-done, bf16[4096,2004]{0,1:T(8,128)(2,1)} %param.9), kind=kOutput, calls=%fused_computation.23 | convolution fusion | flops 16814873600 | bytes 33017872 | tf_op jit(solution)/shard_map/vtd,dc->vtc/dot_general | solution.py:27
  137.6 39.1 %pmax.14 = f32[4,256]{1,0:T(4,128)S(1)} all-reduce(f32[4,256]{1,0:T(4,128)S(1)} %get-tuple-element.7), channel_id=1, replica_groups=mesh['variant'=4,'vocab'=8] {'variant','vocab'}, use_global_device_ids=true, to_apply=%region_2.3 | all-reduce | flops 1024 | bytes 8192 | tf_op jit(solution)/shard_map/pmax | solution.py:31
  176.7 4.4 %fusion.2 = f32[4,256]{1,0:T(4,128)S(1)} fusion(f32[4,256,2004]{1,2,0:T(8,128)} %get-tuple-element.8, f32[4,256]{1,0:T(4,128)S(1)} %pmax.14), kind=kLoop, calls=%fused_computation.5 | loop fusion | flops 4103168 | bytes 8216576 | tf_op jit(solution)/shard_map/reduce_sum | solution.py:32
  181.1 40.6 %psum.28 = f32[4,256]{1,0:T(4,128)S(1)} all-reduce(f32[4,256]{1,0:T(4,128)S(1)} %fusion.2), channel_id=1, replica_groups=mesh['variant'=4,'vocab'=8] {'variant','vocab'}, use_global_device_ids=true, to_apply=%region_4.5 | all-reduce | flops 1024 | bytes 8192 | tf_op jit(solution)/shard_map/psum | solution.py:32
  221.8 4.9 %divide_reduce_fusion = f32[256,2004]{0,1:T(8,128)S(1)} fusion(f32[4,256,2004]{1,2,0:T(8,128)} %get-tuple-element.8, f32[4,256]{1,0:T(4,128)S(1)} %psum.28, f32[4,256]{1,0:T(4,128)S(1)} %pmax.14), kind=kLoop, calls=%fused_computation.3 | loop fusion | flops 5643264 | bytes 10268672 | tf_op jit(solution)/shard_map/reduce_sum | solution.py:34
  226.7 0.0 copy-start.3
  226.7 0.2 multiply_convert_fusion
  226.9 1.5 copy.13
  228.4 3.6 %all-to-all-start = ((bf16[4,64,2004]{2,1,0:T(8,128)(2,1)}), bf16[4,64,2004]{2,1,0:T(8,128)(2,1)S(1)}, u32[]{:S(2)}, u32[]{:S(2)}) async-start(bf16[4,64,2004]{2,1,0:T(8,128)(2,1)} %bitcast.1), calls=%async_computation | async-start | bytes 2097152 | tf_op jit(solution)/shard_map/all_to_all | solution.py:35
  232.0 0.0 all-gather.5.cloned.1.call-start
  232.0 0.0 copy-done.3
  232.1 0.0 reduce-scatter.2.cloned.1.call-done
  232.1 1.8 reduce_max.19
  233.9 13.7 %pmax.15 = f32[64]{0:T(128)S(1)} all-reduce(f32[64]{0:T(128)S(1)} %reduce_max.19), channel_id=1, replica_groups=mesh['variant'=4,'vocab'=8] {'vocab'}, use_global_device_ids=true, to_apply=%region_8.9 | all-reduce | flops 64 | bytes 512 | tf_op jit(solution)/shard_map/pmax | solution.py:46
  247.6 2.0 exponential_reduce_fusion
  249.6 13.8 %psum.29 = f32[64]{0:T(128)S(1)} all-reduce(f32[64]{0:T(128)S(1)} %exponential_reduce_fusion), channel_id=1, replica_groups=mesh['variant'=4,'vocab'=8] {'vocab'}, use_global_device_ids=true, to_apply=%region_10.11 | all-reduce | flops 64 | bytes 512 | tf_op jit(solution)/shard_map/psum | solution.py:47
  263.4 0.0 all-to-all-done
  263.4 0.2 convert_bitcast_fusion
  263.6 0.0 copy-start.1
  263.7 0.0 copy-start.2
  263.7 2.7 copy.14
  266.3 3.9 %reshape.27 = f32[64,8016]{1,0:T(8,128)} reshape(f32[64,4,2004]{2,1,0:T(4,128)} %copy.14) | data formatting | bytes 4104192 | tf_op jit(solution)/shard_map/convert_element_type | solution.py:37
  270.2 0.0 copy-done.1
  270.2 0.0 copy-done.2
  270.2 3.6 %multiply_reduce_fusion = (f32[64]{0:T(128)S(1)}, f32[64]{0:T(128)S(1)}, bf16[64,8016]{1,0:T(8,128)(2,1)}) fusion(f32[64,8016]{1,0:T(8,128)} %reshape.27, f32[64,8016]{1,0:T(8,128)S(1)} %copy-done.1, f32[64]{0:T(128)S(1)} %log_add_fusion, s32[8016]{0:T(1024)S(1)} %iota_add_fusion, s32[64]{0:T(128)S(1)} %copy-done.2, f32[64]{0:T(128)S(1)} %convert_multiply_fusion), kind=kLoop, calls=%fused_computation.14 | loop fusion | flops 6156160 | bytes 5163584 | tf_op jit(solution)/shard_map/reduce_sum | solution.py:55
  273.8 0.0 all-gather.5.cloned.1.call-update
  273.9 13.6 %all-reduce = (f32[64]{0:T(128)S(1)}, f32[64]{0:T(128)S(1)}) all-reduce(f32[64]{0:T(128)S(1)} %get-tuple-element.3, f32[64]{0:T(128)S(1)} %get-tuple-element.2), channel_id=1, replica_groups=mesh['variant'=4,'vocab'=8] {'vocab'}, use_global_device_ids=true, to_apply=%region_14.15 | all-reduce | flops 128 | bytes 1024 | tf_op jit(solution)/shard_map/psum | solution.py:54
  287.5 0.5 subtract_multiply_fusion
  288.0 36.6 %all-gather.5.cloned.1.call-done = bf16[256,8016]{1,0:T(8,128)(2,1)} async-done(((bf16[64,8016]{1,0:T(8,128)(2,1)}), bf16[256,8016]{1,0:T(8,128)(2,1)}) %all-gather.5.cloned.1.call-update) | async-done | bytes 4104208 | tf_op jit(solution)/shard_map/all_gather | solution.py:68
  324.5 10.5 %convolution_bitcast_fusion = f32[512,8016]{0,1:T(8,128)} fusion(bf16[256,8016]{1,0:T(8,128)(2,1)} %all-gather.5.cloned.1.call-done, bf16[256,512]{1,0:T(8,128)(2,1)S(1)} %copy-done), kind=kOutput, calls=%fused_computation.2 | convolution fusion | flops 2101346304 | bytes 20783104 | tf_op jit(solution)/shard_map/dot_general | solution.py:66
  (3 shorter events, 0.0 us)
Async XLA Ops:
  8.0 1.0 copy-start
  8.0 105.6 %all-gather.3.cloned.1.call-start = ((), (), s32[]{:S(2)}) async-start(), calls=%async_computation.2 | async-start | bytes 8650752 | tf_op jit(solution)/shard_map/all_gather | solution.py:25
  8.7 223.3 %reduce-scatter.2.cloned.1.call-start = ((), (), s32[]{:S(2)}) async-start(), calls=%async_computation.3 | async-start | bytes 10321920 | tf_op jit(solution)/shard_map/reduce_scatter | solution.py:39
  18.0 0.7 copy-start.4
  18.0 0.7 copy-start.5
  226.7 5.3 %copy-start.3 = (s32[64]{0:T(128)S(1)}, s32[64]{0:T(128)}, u32[]{:S(2)}) copy-start(s32[64]{0:T(128)} %param.15) | copy-start | bytes 772
  228.4 35.0 %all-to-all-start = ((bf16[4,64,2004]{2,1,0:T(8,128)(2,1)}), bf16[4,64,2004]{2,1,0:T(8,128)(2,1)S(1)}, u32[]{:S(2)}, u32[]{:S(2)}) async-start(bf16[4,64,2004]{2,1,0:T(8,128)(2,1)} %bitcast.1), calls=%async_computation | async-start | bytes 2097152 | tf_op jit(solution)/shard_map/all_to_all | solution.py:35
  232.0 92.5 %all-gather.5.cloned.1.call-start = ((), (), s32[]{:S(2)}) async-start(), calls=%async_computation.4 | async-start | bytes 5160960 | tf_op jit(solution)/shard_map/all_gather | solution.py:68
  263.6 6.6 %copy-start.1 = (f32[64,8016]{1,0:T(8,128)S(1)}, f32[64,8016]{1,0:T(8,128)}, u32[]{:S(2)}) copy-start(f32[64,8016]{1,0:T(8,128)} %reduce-scatter.2.cloned.1.call-done) | copy-start | bytes 6156292
  263.7 6.6 %copy-start.2 = (s32[64]{0:T(128)S(1)}, s32[64]{0:T(128)}, u32[]{:S(2)}) copy-start(s32[64]{0:T(128)} %param.14) | copy-start | bytes 772
Sparse Core Ops, SparseCore 0:
  11.7 101.8 all-gather.2
Sparse Core Ops, SparseCore 1:
  18.1 101.5 reduce-scatter.1
  274.0 50.5 all-gather.4
where the time goes:
time: 343 us
  waiting for transfers between devices  132 us (38%)
  blocking collectives  121 us (35%)
  matrix products  43.6 us (13%)
  other arithmetic  17.9 us (5%)
  between operations  15.6 us (5%)
  local copies, waits for them, and re-layouts  8.88 us (3%)
  starting transfers between devices  3.71 us (1%)
    all_gather x1, waiting for transfers between devices, on_device(): lax.all_gather(teacher_hidden, ('variant', 'vocab'), axis=2, tiled=True)  94.8 us
    psum x1, blocking collectives, on_device(): lax.psum(jnp.sum(jnp.exp(scaled - top[:, :, None]), axis=2), ('variant',...  40.6 us
    pmax x1, blocking collectives, on_device(): top = lax.pmax(local_max, ('variant', 'vocab'))  39.1 us
    all_gather x1, waiting for transfers between devices, on_device(): lax.all_gather(error, 'variant', axis=0, tiled=True)  36.6 us
    dot_general x1, matrix products, on_device(): jnp.einsum('vtd,dc->vtc', hidden_all, teacher_weight, preferred_element_t...  24 us
    psum x1, blocking collectives, on_device(): total = lax.psum(jnp.sum(jnp.exp(logits - top[:, None]), axis=1), 'vocab')  13.8 us
    pmax x1, blocking collectives, on_device(): top = lax.pmax(local_max, 'vocab')  13.7 us
    psum x1, blocking collectives, on_device(): lax.psum((jnp.sum(averaged * log_probs, axis=1), jnp.sum(jnp.where(onehot...  13.6 us
  transfers between devices with their start and end apart: 4, of which 2 were waited for; matrix products, arithmetic and copies ran while one was open for 14% of the time, Pallas kernels for 0%

commit v1 on v0

v1 whole, which is shorter than its diff:
```python
import functools

import jax
import jax.numpy as jnp
from jax import lax
from jax.experimental import pallas as pl
from jax.experimental.pallas import tpu as pltpu
from jax.sharding import PartitionSpec as P

mix_weight = 0.5
loss_scale = 4096.0
MESH = pl.DeviceIdType.MESH


def gather_kernel(h_ref, ids_ref, out_ref, ids_out, send, recv, isend, irecv, local):
    v, w = lax.axis_index("variant"), lax.axis_index("vocab")
    z, c = w // 2, w % 2
    xn = v + 1 - 2 * (v % 2)
    yn = (v + 2) % 4
    dg = (xn + 2) % 4
    sib = w + 1 - 2 * c
    width = h_ref.shape[2]
    half = h_ref.shape[0] // 2

    partners = [(v, ((z + k) % 4) * 2 + c) for k in (1, 2, 3)] + [(xn, w), (yn, w), (dg, w), (v, sib)]
    barrier = pltpu.get_barrier_semaphore()
    for device in partners:
        pl.semaphore_signal(barrier, inc=1, device_id=device, device_id_type=MESH)
    pl.semaphore_wait(barrier, len(partners))

    def block(variant, k, lo=0, n=2 * half):
        column = (variant * 8 + ((z + 4 - k) % 4) * 2 + c) * width
        return out_ref.at[pl.ds(lo, n), :, pl.ds(pl.multiple_of(column, width), width)]

    started = []

    def push(src, dst, device, sem):
        copy = pltpu.make_async_remote_copy(
            src_ref=src, dst_ref=dst, send_sem=send.at[sem], recv_sem=recv.at[sem],
            device_id=device, device_id_type=MESH,
        )
        copy.start()
        started.append(copy)
        return copy

    own = pltpu.make_async_copy(h_ref, block(v, 0), local.at[0])
    own.start()
    own_ids = pltpu.make_async_copy(ids_ref, ids_out.at[v], local.at[1])
    own_ids.start()
    along = {k: push(h_ref, block(v, 0), (v, ((z + k) % 4) * 2 + c), k - 1) for k in (1, 2, 3)}
    id_copies = []
    for i, device in enumerate((xn, yn, dg)):
        copy = pltpu.make_async_remote_copy(
            src_ref=ids_ref, dst_ref=ids_out.at[v], send_sem=isend.at[i], recv_sem=irecv.at[i],
            device_id=(device, w), device_id_type=MESH,
        )
        copy.start()
        id_copies.append(copy)

    over_x, over_y, via_x, via_y, across = {}, {}, {}, {}, []

    def spread(k):
        src = h_ref if k == 0 else block(v, k)
        if k:
            along[k].wait_recv()
        over_x[k] = push(src, block(v, k), (xn, w), 3 + k)
        over_y[k] = push(src, block(v, k), (yn, w), 7 + k)
        across.append(push(src, block(v, k), (v, sib), 19 + k))

    def forward(k):
        over_x[k].wait_recv()
        via_x[k] = push(block(xn, k, 0, half), block(xn, k, 0, half), (yn, w), 11 + k)
        across.append(push(block(xn, k), block(xn, k), (v, sib), 23 + k))
        over_y[k].wait_recv()
        via_y[k] = push(block(yn, k, half, half), block(yn, k, half, half), (xn, w), 15 + k)
        across.append(push(block(yn, k), block(yn, k), (v, sib), 27 + k))

    def last(k):
        via_x[k].wait_recv()
        via_y[k].wait_recv()
        across.append(push(block(dg, k), block(dg, k), (v, sib), 31 + k))

    for k in range(6):
        if k < 4:
            spread(k)
        if 1 <= k < 5:
            forward(k - 1)
        if k >= 2:
            last(k - 2)
    for copy in across:
        copy.wait_recv()
    for copy in started:
        copy.wait_send()
    for copy in id_copies:
        copy.wait()
    own.wait()
    own_ids.wait()


def gather_inputs(hidden, ids, n_devices):
    v, t, d = hidden.shape
    return pl.pallas_call(
        gather_kernel,
        out_shape=(
            jax.ShapeDtypeStruct((v, t, d * n_devices), hidden.dtype),
            jax.ShapeDtypeStruct((4,) + ids.shape, ids.dtype),
        ),
        in_specs=[pl.BlockSpec(memory_space=pl.ANY)] * 2,
        out_specs=[pl.BlockSpec(memory_space=pl.ANY)] * 2,
        scratch_shapes=[
            pltpu.SemaphoreType.DMA((35,)),
            pltpu.SemaphoreType.DMA((35,)),
            pltpu.SemaphoreType.DMA((3,)),
            pltpu.SemaphoreType.DMA((3,)),
            pltpu.SemaphoreType.DMA((2,)),
        ],
        compiler_params=pltpu.CompilerParams(collective_id=0, has_side_effects=True),
    )(hidden, ids)


def merge(parts):
    top = functools.reduce(jnp.maximum, [p[0] for p in parts])
    scales = [jnp.exp(p[0] - top) for p in parts]
    total = sum(p[1] * s for p, s in zip(parts, scales))
    weighted = sum(p[2] * s for p, s in zip(parts, scales))
    return top, total, weighted


def stats_kernel(n1, n2, x_ref, out_ref, got1, mid, got2, s1, r1, s2, r2):
    v, w = lax.axis_index("variant"), lax.axis_index("vocab")
    firsts = [((v + k) % n1, w) for k in range(1, n1)]
    seconds = [(v, (w + k) % n2) for k in range(1, n2)]
    barrier = pltpu.get_barrier_semaphore()
    for device in firsts + seconds:
        pl.semaphore_signal(barrier, inc=1, device_id=device, device_id_type=MESH)
    pl.semaphore_wait(barrier, len(firsts) + len(seconds))

    def exchange(src, got, send, recv, devices):
        copies = []
        for k, device in enumerate(devices):
            copy = pltpu.make_async_remote_copy(
                src_ref=src, dst_ref=got.at[k], send_sem=send.at[k], recv_sem=recv.at[k],
                device_id=device, device_id_type=MESH,
            )
            copy.start()
            copies.append(copy)
        for copy in copies:
            copy.wait()
        return merge([[src[j] for j in range(3)]] + [[got[k, j] for j in range(3)] for k in range(len(devices))])

    for j, value in enumerate(exchange(x_ref, got1, s1, r1, firsts)):
        mid[j] = value
    for j, value in enumerate(exchange(mid, got2, s2, r2, seconds)):
        out_ref[j] = value


def merge_everywhere(stats, n1, n2):
    return pl.pallas_call(
        functools.partial(stats_kernel, n1, n2),
        out_shape=jax.ShapeDtypeStruct(stats.shape, stats.dtype),
        in_specs=[pl.BlockSpec(memory_space=pltpu.VMEM)],
        out_specs=pl.BlockSpec(memory_space=pltpu.VMEM),
        scratch_shapes=[
            pltpu.VMEM((n1 - 1,) + stats.shape, stats.dtype),
            pltpu.VMEM(stats.shape, stats.dtype),
            pltpu.VMEM((n2 - 1,) + stats.shape, stats.dtype),
            pltpu.SemaphoreType.DMA((n1 - 1,)),
            pltpu.SemaphoreType.DMA((n1 - 1,)),
            pltpu.SemaphoreType.DMA((n2 - 1,)),
            pltpu.SemaphoreType.DMA((n2 - 1,)),
        ],
        compiler_params=pltpu.CompilerParams(collective_id=1, has_side_effects=True),
    )(stats)


def on_device(
    teacher_hidden,
    teacher_weight,
    variant_ids,
    temps,
    student_hidden,
    student_weight,
    token_ids,
    loss_mask,
):
    n1, n2 = lax.axis_size("variant"), lax.axis_size("vocab")
    n_variant = teacher_hidden.shape[0]
    columns = teacher_weight.shape[1]
    rows = token_ids.shape[0]
    tokens = rows * n1
    categories = jnp.arange(temps.shape[0], dtype=jnp.int32)
    taus = jnp.sum(
        jnp.where(variant_ids[:, None] == categories[None, :], temps[None, :], 0.0), axis=1
    )
    partial = jnp.dot(student_weight.T, student_hidden.T, preferred_element_type=jnp.float32)
    logits = lax.psum_scatter(
        partial.reshape(n1, columns, tokens), "variant", scatter_dimension=0, tiled=False
    )
    ids = jnp.pad(jnp.stack([token_ids, loss_mask]), ((0, 6), (0, 128 - rows)))
    if (n1, n2) == (4, 8) and teacher_hidden.shape[2] % 128 == 0:
        hidden_all, ids_all = gather_inputs(teacher_hidden, ids, n1 * n2)
    else:
        hidden_all = lax.all_gather(teacher_hidden, ("variant", "vocab"), axis=2, tiled=True)
        ids_all = lax.all_gather(ids, "variant", axis=0)
    token_all = ids_all[:, 0, :rows].reshape(tokens)
    mask_all = ids_all[:, 1, :rows].reshape(tokens).astype(jnp.float32)

    scaled = (
        jnp.einsum("dc,vtd->vct", teacher_weight, hidden_all, preferred_element_type=jnp.float32)
        / taus[:, None, None]
    )
    t_max = jnp.max(scaled, axis=1)
    t_exp = jnp.exp(scaled - t_max[:, None, :])
    t_sum = jnp.sum(t_exp, axis=1)
    t_dot = jnp.sum(t_exp * logits[None], axis=1)
    s_max = jnp.max(logits, axis=0)
    s_sum = jnp.sum(jnp.exp(logits - s_max[None, :]), axis=0)
    here = lax.axis_index("vocab") * (columns * n1) + lax.axis_index("variant") * columns
    onehot = (here + jnp.arange(columns, dtype=jnp.int32))[:, None] == token_all[None, :]
    s_hit = jnp.sum(jnp.where(onehot, logits, 0.0), axis=0)

    zero = jnp.zeros_like(s_max)
    pad = [zero] * (-(n_variant + 2) % 8)
    stats = jnp.stack(
        [
            jnp.stack([t_max[i] for i in range(n_variant)] + [s_max, zero] + pad),
            jnp.stack([t_sum[i] for i in range(n_variant)] + [s_sum, zero] + pad),
            jnp.stack([t_dot[i] for i in range(n_variant)] + [zero, s_hit] + pad),
        ]
    )
    top, total, weighted = merge_everywhere(stats, n1, n2)
    lse = top[n_variant] + jnp.log(total[n_variant])
    hit = weighted[n_variant + 1]
    soft = jnp.sum(weighted[:n_variant] / total[:n_variant], axis=0) / n_variant - lse
    hard = hit - lse
    loss = mask_all * (-mix_weight * soft - (1.0 - mix_weight) * hard)
    token_loss = lax.dynamic_slice(loss, (lax.axis_index("variant") * rows,), (rows,))

    averaged = (
        jnp.sum(
            jnp.exp(scaled - top[:n_variant, None, :]) / total[:n_variant, None, :], axis=0
        )
        / n_variant
    )
    q = jnp.exp(logits - lse[None, :])
    error = (
        loss_scale
        * mask_all[None, :]
        * (q - mix_weight * averaged - (1.0 - mix_weight) * onehot.astype(jnp.float32))
    ).astype(jnp.bfloat16)
    error_all = lax.all_gather(error, "variant", axis=0).reshape(n1 * columns, tokens)
    grad = jnp.dot(error_all, student_hidden, preferred_element_type=jnp.float32)
    return (token_loss, grad.T)


def solution(mesh):
    in_specs = (
        P(None, None, ("variant", "vocab")),
        P(None, ("vocab", "variant")),
        P(),
        P(),
        P(None, "variant"),
        P("variant", "vocab"),
        P("variant"),
        P("variant"),
    )
    out_specs = (P("variant"), P("variant", "vocab"))
    return jax.shard_map(
        on_device, mesh=mesh, in_specs=in_specs, out_specs=out_specs, check_vma=False
    )
```

time: 343 us -> 244 us (0.71)
  blocking collectives: 121 us -> 0 us
  Pallas kernels: 0 us -> 87.5 us
  waiting for transfers between devices: 132 us -> 67.7 us
  local copies, waits for them, and re-layouts: 8.88 us -> 14 us
  starting transfers between devices: 3.71 us -> 0.26 us
    pallas_call x0 -> x2, Pallas kernels: none -> 87.5 us  [the longest x1 75.4 us: gather_inputs(): pl.pallas_call(gather_kernel, out_shape=(jax.ShapeDtypeStruct((v, t, d *...]
    all_gather x2 -> x1, waiting for transfers between devices: 131 us -> 51.9 us  [on_device(): lax.all_gather(error, 'variant', axis=0).reshape(n1 * columns, tokens)]
    psum x3 -> x0, blocking collectives: 68 us -> none  [the longest x1 40.6 us: on_device(): lax.psum(jnp.sum(jnp.exp(scaled - top[:, :, None]), axis=2), ('variant',...]
    pmax x2 -> x0, blocking collectives: 52.8 us -> none  [the longest x1 39.1 us: on_device(): top = lax.pmax(local_max, ('variant', 'vocab'))]
    unnamed x3, waiting for transfers between devices: 0.72 us -> 15.8 us
    reshape x0 -> x2, local copies, waits for them, and re-layouts: none -> 9.8 us  [the longest x1 5.89 us: on_device(): partial.reshape(n1, columns, tokens)]
    convert_element_type x3 -> x1, local copies, waits for them, and re-layouts: 8.05 us -> 0.08 us  [on_device(): mask_all = ids_all[:, 1, :rows].reshape(tokens).astype(jnp.float32)]
    all_to_all x1 -> x0, starting transfers between devices: 3.63 us -> none  [on_device(): lax.all_to_all(averaged_cols.astype(jnp.bfloat16), 'variant', split_axis=...]
  transfers between devices with their start and end apart: 4 -> 2, of which waited for: 2 -> 2; matrix products, arithmetic and copies ran while one was open for 14% -> 11% of each run, Pallas kernels for 0% -> 31%
where the time goes in v1:
time: 244 us; the launch traced here: 243 us
  Pallas kernels  87.5 us (36%)
  waiting for transfers between devices  67.7 us (28%)
  matrix products  43.3 us (18%)
  other arithmetic  16.1 us (7%)
  between operations  14.1 us (6%)
  local copies, waits for them, and re-layouts  14 us (6%)
    pallas_call x1, Pallas kernels, gather_inputs(): pl.pallas_call(gather_kernel, out_shape=(jax.ShapeDtypeStruct((v, t, d *...  75.4 us
    all_gather x1, waiting for transfers between devices, on_device(): lax.all_gather(error, 'variant', axis=0).reshape(n1 * columns, tokens)  51.9 us
    dot_general x1, matrix products, on_device(): jnp.einsum('dc,vtd->vct', teacher_weight, hidden_all, preferred_element_t...  24 us
    unnamed x3, waiting for transfers between devices  15.8 us
    pallas_call x1, Pallas kernels, merge_everywhere(): pl.pallas_call(functools.partial(stats_kernel, n1, n2), out_shape=jax.Sha...  12.1 us
    dot_general x1, matrix products, on_device(): jnp.dot(error_all, student_hidden, preferred_element_type=jnp.float32)  10.5 us
    dot_general x1, matrix products, on_device(): jnp.dot(student_weight.T, student_hidden.T, preferred_element_type=jnp.fl...  8.82 us
    reshape x1, local copies, waits for them, and re-layouts, on_device(): partial.reshape(n1, columns, tokens)  5.89 us
  transfers between devices with their start and end apart: 2, of which 2 were waited for; matrix products, arithmetic and copies ran while one was open for 11% of the time, Pallas kernels for 31%

profile of v1, /device:TPU:0, one launch (start us, length us, event | category | flops | bytes accessed | tf_op | source)
XLA Modules:
  0.0 243.0 jit_solution(5626027243269661723)
XLA Ops:
  7.2 0.0 copy-start
  7.2 0.0 reduce-scatter.4.cloned.1.call-start
  7.2 0.9 copy-done
  8.1 8.8 %fusion.17 = f32[8016,256]{1,0:T(8,128)} fusion(bf16[512,8016]{0,1:T(8,128)(2,1)} %param.13, bf16[256,512]{1,0:T(8,128)(2,1)S(1)} %copy-done), kind=kOutput, calls=%fused_computation.40 | convolution fusion | flops 2101346304 | bytes 16678912 | tf_op jit(solution)/shard_map/dot_general | solution.py:195
  16.9 5.9 %reshape.123 = f32[4,2004,256]{2,1,0:T(8,128)} reshape(f32[8016,256]{1,0:T(8,128)} %fusion.17) | data formatting | bytes 16416768 | tf_op jit(solution)/shard_map/reshape | solution.py:197
  22.8 0.0 copy-start.2
  22.8 0.0 copy-start.3
  22.8 0.0 copy-start.4
  22.8 0.0 copy-start.5
  22.8 0.0 reduce-scatter.4.cloned.1.call-update
  22.9 0.2 all-gather.2.cloned.1.call-start
  23.1 0.4 copy-done.2
  23.5 0.0 copy-done.3
  23.5 0.6 pad.4.ids_ref
  24.1 75.4 %shard_map.95 = (bf16[4,256,4096]{2,1,0:T(8,128)(2,1)}, s32[4,8,128]{2,1,0:T(8,128)}) custom-call(bf16[4,256,128]{2,1,0:T(8,128)(2,1)} %h_ref.1, s32[8,128]{1,0:T(8,128)} %pad.4.ids_ref), custom_call_target="tpu_custom_call" | custom-call | tf_op jit(solution)/shard_map/pallas_call | solution.py:102
  99.5 0.7 slice_reduce_fusion
  100.3 0.1 eq.45
  100.4 0.7 convert_reduce_fusion
  101.1 0.1 convert_element_type.16
  101.2 0.1 pad.19.clone
  101.3 0.0 copy-done.4
  101.3 0.0 copy-done.5
  101.3 0.2 select_reduce_fusion.1
  101.5 24.0 %bitcast_reduce_fusion = (f32[4,256]{1,0:T(4,128)S(1)}, f32[4,256,2004]{1,2,0:T(8,128)}) fusion(f32[4]{0:T(128)S(1)} %select_reduce_fusion.1, bf16[4,256,4096]{2,1,0:T(8,128)(2,1)} %get-tuple-element.5, bf16[4096,2004]{0,1:T(8,128)(2,1)} %param.9), kind=kOutput, calls=%fused_computation.5 | convolution fusion | flops 16814873600 | bytes 33017872 | tf_op jit(solution)/shard_map/dc,vtd->vct/dot_general | solution.py:209
  125.4 15.7 %reduce-scatter.4.cloned.1.call-done = f32[1,2004,256]{2,1,0:T(8,128)} async-done(((f32[4,2004,256]{2,1,0:T(8,128)}), f32[1,2004,256]{2,1,0:T(8,128)}) %reduce-scatter.4.cloned.1.call-update) | async-done | bytes 2052112
  141.2 0.0 copy-start.1
  141.2 4.9 %fusion.6 = (f32[4,256]{1,0:T(4,128)S(1)}, f32[4,256]{1,0:T(4,128)S(1)}) fusion(f32[4,256,2004]{1,2,0:T(8,128)} %get-tuple-element.20, f32[4,256]{1,0:T(4,128)S(1)} %get-tuple-element.19, f32[2004,256]{1,0:T(8,128)} %bitcast.65), kind=kLoop, calls=%fused_computation.11 | loop fusion | flops 8206336 | bytes 10272768 | tf_op jit(solution)/shard_map/reduce_sum | solution.py:214
  146.1 0.0 copy-done.1
  146.1 0.3 reduce_max.19
  146.4 1.0 exponential_reduce_fusion
  147.4 0.1 fusion.13
  147.5 0.6 pad_maximum_fusion.x_ref
  148.1 12.1 %shard_map.96 = f32[3,8,256]{2,1,0:T(8,128)} custom-call(f32[3,8,256]{2,1,0:T(8,128)} %pad_maximum_fusion.x_ref), custom_call_target="tpu_custom_call" | custom-call | tf_op jit(solution)/shard_map/pallas_call | solution.py:158
  160.2 0.7 fusion.16
  160.9 0.7 log_add_fusion
  161.7 0.7 slice_bitcast_fusion
  162.4 4.9 %fusion.5 = f32[2004,256]{1,0:T(8,128)S(1)} fusion(f32[4,256,2004]{1,2,0:T(8,128)} %get-tuple-element.20, f32[4,256]{1,0:T(4,128)S(1)} %get-tuple-element.11, f32[4,256]{1,0:T(4,128)S(1)} %get-tuple-element.10), kind=kLoop, calls=%fused_computation.10 | loop fusion | flops 5643264 | bytes 10268672 | tf_op jit(solution)/shard_map/reduce_sum | solution.py:240
  167.3 1.9 fusion.11
  169.2 0.0 all-gather.2.cloned.1.call-update
  169.2 0.6 dynamic_slice.3
  169.8 51.9 %all-gather.2.cloned.1.call-done = bf16[4,2004,256]{2,1,0:T(8,128)(2,1)} async-done(((bf16[1,2004,256]{2,1,0:T(8,128)(2,1)}), bf16[4,2004,256]{2,1,0:T(8,128)(2,1)}) %all-gather.2.cloned.1.call-update) | async-done | bytes 4104208 | tf_op jit(solution)/shard_map/all_gather | solution.py:251
  221.7 3.9 %reshape.124 = bf16[8016,256]{1,0:T(8,128)(2,1)} reshape(bf16[4,2004,256]{2,1,0:T(8,128)(2,1)} %all-gather.2.cloned.1.call-done) | data formatting | bytes 8208384 | tf_op jit(solution)/shard_map/reshape | solution.py:251
  225.6 10.5 %convolution_bitcast_fusion = f32[512,8016]{0,1:T(8,128)} fusion(bf16[8016,256]{1,0:T(8,128)(2,1)} %reshape.124, bf16[256,512]{1,0:T(8,128)(2,1)S(1)} %copy-done), kind=kOutput, calls=%fused_computation.2 | convolution fusion | flops 2101346304 | bytes 20783104 | tf_op jit(solution)/shard_map/dot_general | solution.py:252
  (5 shorter events, 0.0 us)
Async XLA Ops:
  7.2 1.0 copy-start
  7.2 134.0 %reduce-scatter.4.cloned.1.call-start = ((), (), s32[]{:S(2)}) async-start(), calls=%async_computation.2 | async-start | bytes 10280960
  22.8 0.7 copy-start.2
  22.8 0.7 copy-start.3
  22.8 78.4 %copy-start.4 = (f32[14]{0:T(128)S(1)}, f32[14]{0:T(128)}, u32[]{:S(2)}) copy-start(f32[14]{0:T(128)} %param.11) | copy-start | bytes 172
  22.8 78.4 %copy-start.5 = (s32[4]{0:T(128)S(1)}, s32[4]{0:T(128)}, u32[]{:S(2)}) copy-start(s32[4]{0:T(128)} %param.10) | copy-start | bytes 52
  22.9 198.9 %all-gather.2.cloned.1.call-start = ((), (), s32[]{:S(2)}) async-start(), calls=%async_computation.1 | async-start | bytes 5140480 | tf_op jit(solution)/shard_map/all_gather | solution.py:251
  141.2 4.9 %copy-start.1 = (f32[1,2004,256]{2,1,0:T(8,128)S(1)}, f32[1,2004,256]{2,1,0:T(8,128)}, u32[]{:S(2)}) copy-start(f32[1,2004,256]{2,1,0:T(8,128)} %reduce-scatter.4.cloned.1.call-done) | copy-start | bytes 6156292
Sparse Core Ops, SparseCore 0:
  23.0 118.1 reduce-scatter.3
  169.4 52.3 all-gather.1

commit v2 on v1

--- a/solution.py
+++ b/solution.py
@@ -173,6 +173,63 @@
     )(stats)
 
 
+def error_kernel(e_ref, out_ref, send, recv, local):
+    v, w = lax.axis_index("variant"), lax.axis_index("vocab")
+    xn = v + 1 - 2 * (v % 2)
+    yn = (v + 2) % 4
+    barrier = pltpu.get_barrier_semaphore()
+    for device in (xn, yn):
+        pl.semaphore_signal(barrier, inc=1, device_id=(device, w), device_id_type=MESH)
+    pl.semaphore_wait(barrier, 2)
+
+    half = e_ref.shape[1] // 2
+
+    def part(variant, i):
+        return out_ref.at[variant, :, pl.ds(i * half, half)]
+
+    def push(src, dst, device, sem):
+        copy = pltpu.make_async_remote_copy(
+            src_ref=src, dst_ref=dst, send_sem=send.at[sem], recv_sem=recv.at[sem],
+            device_id=(device, w), device_id_type=MESH,
+        )
+        copy.start()
+        return copy
+
+    mine = [e_ref.at[:, pl.ds(i * half, half)] for i in range(2)]
+    x0 = push(mine[0], part(v, 0), xn, 0)
+    y1 = push(mine[1], part(v, 1), yn, 1)
+    x1 = push(mine[1], part(v, 1), xn, 2)
+    y0 = push(mine[0], part(v, 0), yn, 3)
+    own = pltpu.make_async_copy(e_ref, out_ref.at[v], local.at[0])
+    own.start()
+    x0.wait_recv()
+    via_x = push(part(xn, 0), part(xn, 0), yn, 4)
+    y1.wait_recv()
+    via_y = push(part(yn, 1), part(yn, 1), xn, 5)
+    x1.wait_recv()
+    y0.wait_recv()
+    via_x.wait_recv()
+    via_y.wait_recv()
+    for copy in (x0, y1, x1, y0, via_x, via_y):
+        copy.wait_send()
+    own.wait()
+
+
+def gather_errors(error):
+    return pl.pallas_call(
+        error_kernel,
+        out_shape=jax.ShapeDtypeStruct((4,) + error.shape, error.dtype),
+        in_specs=[pl.BlockSpec(memory_space=pl.ANY)],
+        out_specs=pl.BlockSpec(memory_space=pl.ANY),
+        scratch_shapes=[
+            pltpu.SemaphoreType.DMA((6,)),
+            pltpu.SemaphoreType.DMA((6,)),
+            pltpu.SemaphoreType.DMA((1,)),
+        ],
+        compiler_params=pltpu.CompilerParams(collective_id=2, has_side_effects=True),
+    )(error)
+
+
 def on_device(
     teacher_hidden,
     teacher_weight,
@@ -248,7 +305,11 @@
         * mask_all[None, :]
         * (q - mix_weight * averaged - (1.0 - mix_weight) * onehot.astype(jnp.float32))
     ).astype(jnp.bfloat16)
-    error_all = lax.all_gather(error, "variant", axis=0).reshape(n1 * columns, tokens)
+    if (n1, n2) == (4, 8) and tokens % 256 == 0:
+        error_all = gather_errors(error)
+    else:
+        error_all = lax.all_gather(error, "variant", axis=0)
+    error_all = error_all.reshape(n1 * columns, tokens)
     grad = jnp.dot(error_all, student_hidden, preferred_element_type=jnp.float32)
     return (token_loss, grad.T)
 

time: 244 us -> 228 us (0.934)
  waiting for transfers between devices: 67.7 us -> 15.8 us
  Pallas kernels: 87.5 us -> 124 us
    all_gather x1 -> x0, waiting for transfers between devices: 51.9 us -> none  [on_device(): lax.all_gather(error, 'variant', axis=0).reshape(n1 * columns, tokens)]
    pallas_call x0 -> x1, Pallas kernels: none -> 36.5 us  [gather_errors(): pl.pallas_call(error_kernel, out_shape=jax.ShapeDtypeStruct((4,) + error....]
    unnamed x3 -> x2, waiting for transfers between devices: 15.8 us -> 15.8 us
  transfers between devices with their start and end apart: 2 -> 1, of which waited for: 2 -> 1; matrix products, arithmetic and copies ran while one was open for 11% -> 12% of each run, Pallas kernels for 31% -> 33%
where the time goes in v2:
time: 228 us
  Pallas kernels  124 us (54%)
  matrix products  43.3 us (19%)
  other arithmetic  16.1 us (7%)
  waiting for transfers between devices  15.8 us (7%)
  local copies, waits for them, and re-layouts  14.2 us (6%)
  between operations  14.1 us (6%)
    pallas_call x1, Pallas kernels, gather_inputs(): pl.pallas_call(gather_kernel, out_shape=(jax.ShapeDtypeStruct((v, t, d *...  75.4 us
    pallas_call x1, Pallas kernels, gather_errors(): pl.pallas_call(error_kernel, out_shape=jax.ShapeDtypeStruct((4,) + error....  36.5 us
    dot_general x1, matrix products, on_device(): jnp.einsum('dc,vtd->vct', teacher_weight, hidden_all, preferred_element_t...  24 us
    unnamed x2, waiting for transfers between devices  15.8 us
    pallas_call x1, Pallas kernels, merge_everywhere(): pl.pallas_call(functools.partial(stats_kernel, n1, n2), out_shape=jax.Sha...  12.1 us
    dot_general x1, matrix products, on_device(): jnp.dot(error_all, student_hidden, preferred_element_type=jnp.float32)  10.5 us
    dot_general x1, matrix products, on_device(): jnp.dot(student_weight.T, student_hidden.T, preferred_element_type=jnp.fl...  8.82 us
    reshape x1, local copies, waits for them, and re-layouts, on_device(): partial.reshape(n1, columns, tokens)  5.9 us
  transfers between devices with their start and end apart: 1, of which 1 were waited for; matrix products, arithmetic and copies ran while one was open for 12% of the time, Pallas kernels for 33%

profile of v2, /device:TPU:0, one launch (start us, length us, event | category | flops | bytes accessed | tf_op | source)
XLA Modules:
  0.0 227.6 jit_solution(15605172521666355245)
XLA Ops:
  7.2 0.0 copy-start
  7.2 0.0 reduce-scatter.4.cloned.1.call-start
  7.2 0.9 copy-done
  8.1 8.8 %fusion.18 = f32[8016,256]{1,0:T(8,128)} fusion(bf16[512,8016]{0,1:T(8,128)(2,1)} %param.13, bf16[256,512]{1,0:T(8,128)(2,1)S(1)} %copy-done), kind=kOutput, calls=%fused_computation.41 | convolution fusion | flops 2101346304 | bytes 16678912 | tf_op jit(solution)/shard_map/dot_general | solution.py:252
  16.9 5.9 %reshape.53 = f32[4,2004,256]{2,1,0:T(8,128)} reshape(f32[8016,256]{1,0:T(8,128)} %fusion.18) | data formatting | bytes 16416768 | tf_op jit(solution)/shard_map/reshape | solution.py:254
  22.8 0.0 copy-start.2
  22.8 0.0 copy-start.3
  22.8 0.0 copy-start.4
  22.8 0.0 copy-start.5
  22.8 0.0 reduce-scatter.4.cloned.1.call-update
  22.9 0.6 copy-done.2
  23.5 0.0 copy-done.3
  23.5 0.6 pad.4.ids_ref
  24.1 75.4 %shard_map.95 = (bf16[4,256,4096]{2,1,0:T(8,128)(2,1)}, s32[4,8,128]{2,1,0:T(8,128)}) custom-call(bf16[4,256,128]{2,1,0:T(8,128)(2,1)} %h_ref.1, s32[8,128]{1,0:T(8,128)} %pad.4.ids_ref), custom_call_target="tpu_custom_call" | custom-call | tf_op jit(solution)/shard_map/pallas_call | solution.py:102
  99.5 0.7 slice_reduce_fusion
  100.3 0.1 eq.32
  100.4 0.7 convert_reduce_fusion
  101.1 0.1 convert_element_type.15
  101.2 0.1 pad.19.clone
  101.3 0.0 copy-done.4
  101.3 0.0 copy-done.5
  101.3 0.2 select_reduce_fusion
  101.5 24.0 %bitcast_reduce_fusion = (f32[4,256]{1,0:T(4,128)S(1)}, f32[4,256,2004]{1,2,0:T(8,128)}) fusion(f32[4]{0:T(128)S(1)} %select_reduce_fusion, bf16[4,256,4096]{2,1,0:T(8,128)(2,1)} %get-tuple-element.5, bf16[4096,2004]{0,1:T(8,128)(2,1)} %param.9), kind=kOutput, calls=%fused_computation.5 | convolution fusion | flops 16814873600 | bytes 33017872 | tf_op jit(solution)/shard_map/dc,vtd->vct/dot_general | solution.py:266
  125.4 15.7 %reduce-scatter.4.cloned.1.call-done = f32[1,2004,256]{2,1,0:T(8,128)} async-done(((f32[4,2004,256]{2,1,0:T(8,128)}), f32[1,2004,256]{2,1,0:T(8,128)}) %reduce-scatter.4.cloned.1.call-update) | async-done | bytes 2052112
  141.2 0.0 copy-start.1
  141.2 4.9 %fusion.6 = (f32[4,256]{1,0:T(4,128)S(1)}, f32[4,256]{1,0:T(4,128)S(1)}) fusion(f32[4,256,2004]{1,2,0:T(8,128)} %get-tuple-element.20, f32[4,256]{1,0:T(4,128)S(1)} %get-tuple-element.19, f32[2004,256]{1,0:T(8,128)} %bitcast.58), kind=kLoop, calls=%fused_computation.11 | loop fusion | flops 8206336 | bytes 10272768 | tf_op jit(solution)/shard_map/reduce_sum | solution.py:271
  146.1 0.0 copy-done.1
  146.1 0.3 reduce_max.19
  146.4 1.0 exponential_reduce_fusion
  147.4 0.1 fusion.14
  147.5 0.6 pad_maximum_fusion.x_ref
  148.1 12.1 %shard_map.96 = f32[3,8,256]{2,1,0:T(8,128)} custom-call(f32[3,8,256]{2,1,0:T(8,128)} %pad_maximum_fusion.x_ref), custom_call_target="tpu_custom_call" | custom-call | tf_op jit(solution)/shard_map/pallas_call | solution.py:158
  160.2 0.7 fusion.17
  160.9 0.7 log_add_fusion
  161.7 0.7 slice_bitcast_fusion
  162.4 4.9 %fusion.5 = f32[2004,256]{1,0:T(8,128)S(1)} fusion(f32[4,256,2004]{1,2,0:T(8,128)} %get-tuple-element.20, f32[4,256]{1,0:T(4,128)S(1)} %get-tuple-element.11, f32[4,256]{1,0:T(4,128)S(1)} %get-tuple-element.10), kind=kLoop, calls=%fused_computation.10 | loop fusion | flops 5643264 | bytes 10268672 | tf_op jit(solution)/shard_map/reduce_sum | solution.py:297
  167.3 1.9 fusion.12.e_ref
  169.2 36.5 %shard_map.97 = bf16[4,2004,256]{2,1,0:T(8,128)(2,1)} custom-call(bf16[2004,256]{1,0:T(8,128)(2,1)} %fusion.12.e_ref), custom_call_target="tpu_custom_call" | custom-call | tf_op jit(solution)/shard_map/pallas_call | solution.py:219
  205.7 3.9 %reshape.54 = bf16[8016,256]{1,0:T(8,128)(2,1)} reshape(bf16[4,2004,256]{2,1,0:T(8,128)(2,1)} %shard_map.97) | data formatting | bytes 8208384 | tf_op jit(solution)/shard_map/reshape | solution.py:312
  209.6 10.5 %convolution_bitcast_fusion = f32[512,8016]{0,1:T(8,128)} fusion(bf16[8016,256]{1,0:T(8,128)(2,1)} %reshape.54, bf16[256,512]{1,0:T(8,128)(2,1)S(1)} %copy-done), kind=kOutput, calls=%fused_computation.2 | convolution fusion | flops 2101346304 | bytes 20783104 | tf_op jit(solution)/shard_map/dot_general | solution.py:313
  220.1 0.6 dynamic_slice.3
  (5 shorter events, 0.0 us)
Async XLA Ops:
  7.2 1.0 copy-start
  7.2 134.0 %reduce-scatter.4.cloned.1.call-start = ((), (), s32[]{:S(2)}) async-start(), calls=%async_computation.1 | async-start | bytes 10280960
  22.8 0.7 copy-start.2
  22.8 0.7 copy-start.3
  22.8 78.4 %copy-start.4 = (f32[14]{0:T(128)S(1)}, f32[14]{0:T(128)}, u32[]{:S(2)}) copy-start(f32[14]{0:T(128)} %param.11) | copy-start | bytes 172
  22.8 78.4 %copy-start.5 = (s32[4]{0:T(128)S(1)}, s32[4]{0:T(128)}, u32[]{:S(2)}) copy-start(s32[4]{0:T(128)} %param.10) | copy-start | bytes 52
  141.2 4.9 %copy-start.1 = (f32[1,2004,256]{2,1,0:T(8,128)S(1)}, f32[1,2004,256]{2,1,0:T(8,128)}, u32[]{:S(2)}) copy-start(f32[1,2004,256]{2,1,0:T(8,128)} %reduce-scatter.4.cloned.1.call-done) | copy-start | bytes 6156292
Sparse Core Ops, SparseCore 0:
  23.0 118.1 reduce-scatter.3
